TPU v7x, 32 devices: a whole 2x2x4 slice. The times are simulated.
32 devices in a mesh: grp: 1, feat: 32 (over z, y, x, core), dp: 1.
Axes of the slice: x: 2, y: 2, z: 4, core: 2. Of those that a mesh axis runs over, the one named last changes fastest.
Arguments:
- archive: bfloat16 [1024, 65536], P('grp', 'feat'), may hold values from -6 to 6
- picks: int32 [512], P(('grp', 'dp')), may hold values from 0 to 1023
- first_factor: bfloat16 [256, 256, 256], P(('grp', 'feat')), may hold values from -0.375 to 0.375
- second_factor: bfloat16 [256, 256, 256], P(('grp', 'feat')), may hold values from -0.375 to 0.375
- targets: bfloat16 [512, 65536], P(('grp', 'dp'), 'feat'), may hold values from -6 to 6
Outputs:
- first_grad: float32 [256, 256, 256], P(('grp', 'feat'), 'dp')
- second_grad: float32 [256, 256, 256], P(('grp', 'feat'), 'dp')
All inputs are finite; a program needn't handle non-finite values.
Results may differ from a plain program's by a relative error of at most 0.0095.
Values may be sent and summed in bfloat16 or wider, within the bound.
A program may use at most 64 MiB of HBM per device.

v0:
```python
import math

import jax
import jax.numpy as jnp
from jax import lax
from jax.sharding import PartitionSpec as P


def local(archive, picks, first_factor, second_factor, targets):
    rows = picks.shape[0]
    local_blocks = first_factor.shape[0]
    width = first_factor.shape[1]
    scale = 1.0 / math.sqrt(rows * lax.axis_size("dp"))
    x = jnp.take(archive, picks, axis=0).reshape(rows, local_blocks, width)
    y_first = jnp.einsum(
        "sia,iab->ibs", x, first_factor, preferred_element_type=jnp.float32
    ).astype(jnp.bfloat16)
    z = lax.all_to_all(y_first, "feat", split_axis=1, concat_axis=0, tiled=True)
    z_float = z.astype(jnp.float32)
    hidden = jax.nn.gelu(z_float).astype(jnp.bfloat16)
    pred = jnp.einsum("ijs,jik->sjk", hidden, second_factor, preferred_element_type=jnp.float32)
    goal = targets.reshape(rows, local_blocks, width).astype(jnp.float32)
    resid = ((pred - goal) * scale).astype(jnp.bfloat16)
    grad_two = jnp.einsum("ijs,sjk->jik", hidden, resid, preferred_element_type=jnp.float32)
    half = width // lax.axis_size("dp")
    offset = lax.axis_index("dp") * half
    summed_two = lax.psum(grad_two.astype(jnp.bfloat16), "dp").astype(jnp.float32)
    grad_two = lax.dynamic_slice_in_dim(summed_two, offset, half, 1)
    d_hidden = jnp.einsum("sjk,jik->ijs", resid, second_factor, preferred_element_type=jnp.float32)
    d_z = jax.vjp(jax.nn.gelu, z_float)[1](d_hidden)[0].astype(jnp.bfloat16)
    d_first = lax.all_to_all(d_z, "feat", split_axis=0, concat_axis=1, tiled=True)
    grad_one = jnp.einsum("sia,ibs->iab", x, d_first, preferred_element_type=jnp.float32)
    summed_one = lax.psum(grad_one.astype(jnp.bfloat16), "dp").astype(jnp.float32)
    grad_one = lax.dynamic_slice_in_dim(summed_one, offset, half, 1)
    return (grad_one, grad_two)


def solution(mesh):
    return jax.shard_map(
        local,
        mesh=mesh,
        in_specs=(
            P("grp", "feat"),
            P(("grp", "dp")),
            P(("grp", "feat"), None, None),
            P(("grp", "feat"), None, None),
            P(("grp", "dp"), "feat"),
        ),
        out_specs=(P(("grp", "feat"), "dp", None), P(("grp", "feat"), "dp", None)),
        check_vma=False,
    )
```

profile of v0, /device:TPU:0, one launch (start us, length us, event | category | flops | bytes accessed | tf_op | source)
XLA Modules:
  0.0 152.0 jit_solution(11059374241292626368)
XLA Ops:
  0.6 0.0 copy-start
  0.6 0.8 compare_and_fusion
  1.4 0.7 compare_select_fusion
  2.1 7.1 %gather_fusion = bf16[512,2048]{1,0:T(8,128)(2,1)S(1)} fusion(bf16[1024,2048]{1,0:T(8,128)(2,1)} %param.5, s32[1024]{0:T(1024)S(1)} %pad_clamp_fusion), kind=kCustom, calls=%fused_computation | custom fusion | bytes 4196352 | tf_op jit(solution)/shard_map/jit(_take)/gather | solution.py:14
  9.3 2.5 %copy.45 = bf16[512,2048]{0,1:T(8,128)(2,1)} copy(bf16[512,2048]{1,0:T(8,128)(2,1)S(1)} %gather_fusion) | data formatting | bytes 4194304 | tf_op jit(solution)/shard_map/jit(_take)/gather | solution.py:14
  11.8 2.7 %convert_bitcast_fusion.1 = bf16[8,256,512]{1,2,0:T(8,128)(2,1)S(1)} fusion(bf16[8,256,256]{2,1,0:T(8,128)(2,1)} %param.7, bf16[512,8,256]{0,2,1:T(8,128)(2,1)} %bitcast.47, pred[512]{0:T(512)(128)(4,1)S(1)} %compare_and_fusion), kind=kOutput, calls=%fused_computation.23 | convolution fusion | flops 538968064 | bytes 5243392 | tf_op jit(solution)/shard_map/sia,iab->ibs/dot_general | solution.py:15
  14.5 3.1 %copy.29 = bf16[8,256,512]{2,0,1:T(8,128)(2,1)} copy(bf16[8,256,512]{1,2,0:T(8,128)(2,1)S(1)} %convert_bitcast_fusion.1) | data formatting | bytes 4194304 | tf_op jit(solution)/shard_map/convert_element_type | solution.py:17
  17.5 7.3 %all-to-all-start = ((bf16[8,256,512]{2,0,1:T(8,128)(2,1)}), bf16[8,256,512]{2,0,1:T(8,128)(2,1)S(1)}, u32[]{:S(2)}, u32[]{:S(2)}) async-start(bf16[8,256,512]{2,0,1:T(8,128)(2,1)} %copy.29), calls=%async_computation | async-start | bytes 4194304 | tf_op jit(solution)/shard_map/all_to_all | solution.py:18
  24.8 3.9 %copy.37 = bf16[512,2048]{0,1:T(8,128)(2,1)} copy(bf16[512,2048]{1,0:T(8,128)(2,1)} %param.9) | data formatting | bytes 4194304 | tf_op args[4]
  28.8 4.1 %copy.38 = f32[512,8,256]{2,0,1:T(8,128)} copy(bf16[512,8,256]{0,2,1:T(8,128)(2,1)} %bitcast.46) | data formatting | bytes 6291456 | tf_op jit(solution)/shard_map/convert_element_type | solution.py:22
  32.9 40.9 %all-to-all-done = bf16[8,256,512]{2,0,1:T(8,128)(2,1)S(1)} async-done(((bf16[8,256,512]{2,0,1:T(8,128)(2,1)}), bf16[8,256,512]{2,0,1:T(8,128)(2,1)S(1)}, u32[]{:S(2)}, u32[]{:S(2)}) %all-to-all-start) | async-done | bytes 2097184 | tf_op jit(solution)/shard_map/all_to_all | solution.py:18
  73.7 0.7 convert_bitcast_fusion
  74.4 2.6 %copy.31 = f32[32,8,8,512]{3,2,1,0:T(8,128)} copy(f32[32,8,8,512]{3,2,0,1:T(8,128)S(1)} %convert_bitcast_fusion) | data formatting | bytes 8388608 | tf_op jit(solution)/shard_map/convert_element_type | solution.py:19
  77.0 5.3 %copy.36 = f32[256,8,512]{0,2,1:T(8,128)} copy(f32[256,8,512]{2,1,0:T(8,128)} %bitcast.45) | data formatting | bytes 8388608 | tf_op jit(solution)/shard_map/convert_element_type | solution.py:19
  82.3 0.0 copy-done
  82.3 0.0 copy-start.1
  82.3 5.3 %fusion.11 = bf16[512,8,256]{2,0,1:T(8,128)(2,1)S(1)} fusion(f32[512,8,256]{2,0,1:T(8,128)} %copy.38, bf16[8,256,256]{2,1,0:T(8,128)(2,1)S(1)} %copy-done, f32[256,8,512]{0,2,1:T(8,128)} %copy.36), kind=kOutput, calls=%fused_computation.18 | convolution fusion | flops 549453824 | bytes 11534336 | tf_op jit(solution)/shard_map/ijs,jik->sjk/dot_general | solution.py:21
  87.6 0.0 copy-start.3
  87.6 1.3 copy-done.3
  88.9 0.0 copy-done.1
  88.9 3.2 %fusion.6 = bf16[256,8,512]{0,2,1:T(8,128)(2,1)S(1)} fusion(f32[256,8,512]{0,2,1:T(8,128)S(1)} %copy-done.1, bf16[512,8,256]{2,0,1:T(8,128)(2,1)S(1)} %fusion.11, bf16[8,256,256]{2,1,0:T(8,128)(2,1)S(1)} %copy-done), kind=kOutput, calls=%fused_computation.9 | convolution fusion | flops 557842432 | bytes 9437184 | tf_op jit(solution)/shard_map/sjk,jik->ijs/dot_general | solution.py:29
  92.2 3.2 %copy.40 = bf16[256,8,512]{2,1,0:T(8,128)(2,1)} copy(bf16[256,8,512]{0,2,1:T(8,128)(2,1)S(1)} %fusion.6) | data formatting | bytes 4194304 | tf_op jit(solution)/shard_map/convert_element_type | solution.py:30
  95.3 4.1 %all-to-all-start.1 = ((bf16[256,8,512]{2,1,0:T(8,128)(2,1)}), bf16[256,8,512]{2,1,0:T(8,128)(2,1)}, u32[]{:S(2)}, u32[]{:S(2)}) async-start(bf16[256,8,512]{2,1,0:T(8,128)(2,1)} %copy.40), calls=%async_computation.1 | async-start | bytes 4194304 | tf_op jit(solution)/shard_map/all_to_all | solution.py:31
  99.5 0.0 copy-start.2
  99.5 6.0 %fusion.21 = f32[8,256,256]{2,1,0:T(8,128)} fusion(bf16[512,8,256]{2,0,1:T(8,128)(2,1)} %copy-done.3, f32[256,8,512]{0,2,1:T(8,128)} %copy.36), kind=kOutput, calls=%fused_computation.28 | convolution fusion | flops 547356672 | bytes 8388608 | tf_op jit(solution)/shard_map/ijs,sjk->jik/dot_general | solution.py:24
  105.5 42.9 %all-to-all-done.1 = bf16[256,8,512]{2,1,0:T(8,128)(2,1)} async-done(((bf16[256,8,512]{2,1,0:T(8,128)(2,1)}), bf16[256,8,512]{2,1,0:T(8,128)(2,1)}, u32[]{:S(2)}, u32[]{:S(2)}) %all-to-all-start.1) | async-done | bytes 2097184 | tf_op jit(solution)/shard_map/all_to_all | solution.py:31
  148.4 0.0 copy-done.2
  148.4 3.7 %fusion.18 = f32[8,256,256]{2,1,0:T(8,128)} fusion(bf16[8,32,8,512]{3,2,0,1:T(8,128)(2,1)} %bitcast.9, bf16[512,8,256]{0,2,1:T(8,128)(2,1)S(1)} %bitcast.48, pred[512]{0:T(512)(128)(4,1)S(1)} %compare_and_fusion), kind=kOutput, calls=%fused_computation.26 | convolution fusion | flops 538968064 | bytes 6291968 | tf_op jit(solution)/shard_map/sia,ibs->iab/dot_general | solution.py:32
  (1 shorter events, 0.0 us)
Async XLA Ops:
  0.6 81.6 %copy-start = (bf16[8,256,256]{2,1,0:T(8,128)(2,1)S(1)}, bf16[8,256,256]{2,1,0:T(8,128)(2,1)}, u32[]{:S(2)}) copy-start(bf16[8,256,256]{2,1,0:T(8,128)(2,1)} %param.8) | copy-start | bytes 3145732
  17.5 56.2 %all-to-all-start = ((bf16[8,256,512]{2,0,1:T(8,128)(2,1)}), bf16[8,256,512]{2,0,1:T(8,128)(2,1)S(1)}, u32[]{:S(2)}, u32[]{:S(2)}) async-start(bf16[8,256,512]{2,0,1:T(8,128)(2,1)} %copy.29), calls=%async_computation | async-start | bytes 4194304 | tf_op jit(solution)/shard_map/all_to_all | solution.py:18
  82.3 6.7 %copy-start.1 = (f32[256,8,512]{0,2,1:T(8,128)S(1)}, f32[256,8,512]{0,2,1:T(8,128)}, u32[]{:S(2)}) copy-start(f32[256,8,512]{0,2,1:T(8,128)} %copy.36) | copy-start | bytes 12582916
  87.6 1.4 copy-start.3
  95.3 53.0 %all-to-all-start.1 = ((bf16[256,8,512]{2,1,0:T(8,128)(2,1)}), bf16[256,8,512]{2,1,0:T(8,128)(2,1)}, u32[]{:S(2)}, u32[]{:S(2)}) async-start(bf16[256,8,512]{2,1,0:T(8,128)(2,1)} %copy.40), calls=%async_computation.1 | async-start | bytes 4194304 | tf_op jit(solution)/shard_map/all_to_all | solution.py:31
  99.5 48.9 %copy-start.2 = (bf16[512,2048]{0,1:T(8,128)(2,1)S(1)}, bf16[512,2048]{0,1:T(8,128)(2,1)}, u32[]{:S(2)}) copy-start(bf16[512,2048]{0,1:T(8,128)(2,1)} %copy.45) | copy-start | bytes 6291460
where the time goes:
time: 153 us; the launch traced here: 152 us
  waiting for transfers between devices  83.7 us (55%)
  local copies, waits for them, and re-layouts  33.2 us (22%)
  matrix products  20.9 us (14%)
  starting transfers between devices  11.4 us (7%)
  other arithmetic  2.15 us (1%)
    all_to_all x1, waiting for transfers between devices, local(): lax.all_to_all(d_z, 'feat', split_axis=0, concat_axis=1, tiled=True)  42.9 us
    all_to_all x1, waiting for transfers between devices, local(): z = lax.all_to_all(y_first, 'feat', split_axis=1, concat_axis=0, tiled=True)  40.9 us
    gather x2, local copies, waits for them, and re-layouts, local(): x = jnp.take(archive, picks, axis=0).reshape(rows, local_blocks, width)  9.64 us
    convert_element_type x2, local copies, waits for them, and re-layouts, local(): z_float = z.astype(jnp.float32)  7.86 us
    all_to_all x1, starting transfers between devices, local(): z = lax.all_to_all(y_first, 'feat', split_axis=1, concat_axis=0, tiled=True)  7.3 us
    dot_general x1, matrix products, local(): jnp.einsum('ijs,sjk->jik', hidden, resid, preferred_element_type=jnp.floa...  6.01 us
    dot_general x1, matrix products, local(): jnp.einsum('ijs,jik->sjk', hidden, second_factor, preferred_element_type=...  5.31 us
    unnamed x9, local copies, waits for them, and re-layouts  5.3 us
  transfers between devices with their start and end apart: 2, of which 2 were waited for; matrix products, arithmetic and copies ran while one was open for 9% of the time, Pallas kernels for 0%

commit v1 on v0

v1 whole, which is shorter than its diff:
```python
import functools
import math

import jax
import jax.numpy as jnp
from jax import lax
from jax.experimental import pallas as pl
from jax.experimental.pallas import tpu as pltpu
from jax.sharding import PartitionSpec as P

BF16 = jnp.bfloat16
F32 = jnp.float32
CH = 128
ROOT = math.sqrt(2.0 / math.pi)
CUBE = 0.044715


def dot(a, b, ca, cb):
    return lax.dot_general(a, b, (((ca,), (cb,)), ((), ())), preferred_element_type=F32)


def flip(me, k, n):
    out = 0
    bit = 1
    while bit < n:
        out = out + ((me // bit + k // bit) % 2) * bit
        bit *= 2
    return out


def kernel(n, lb, scale, picks, arch_hbm, f1_hbm, f2_hbm, goal_hbm, g1_hbm, g2_hbm,
           arch, f1, f2, goal, f1t, xc, xt, send, recv, bsend, brecv, zbuf, dzbuf, g1, g2,
           in_sem, out_sem, send_sem, recv_sem, bsend_sem, brecv_sem):
    me = lax.axis_index("feat")
    width = n * lb
    rows = goal.shape[0]
    chunks = rows // CH
    patterns = arch.shape[0]
    cell = lb * lb
    per = width // cell
    groups = n // per
    part = per * lb

    loads = [
        pltpu.make_async_copy(src, dst, in_sem.at[t])
        for t, (src, dst) in enumerate(((f1_hbm, f1), (arch_hbm, arch), (f2_hbm, f2), (goal_hbm, goal)))
    ]
    for load in loads:
        load.start()

    barrier = pltpu.get_barrier_semaphore()

    def greet(k, carry):
        pl.semaphore_signal(barrier, inc=1, device_id={"feat": flip(me, k, n)}, device_id_type=pl.DeviceIdType.MESH)
        return carry

    lax.fori_loop(1, n, greet, 0)

    left = lax.broadcasted_iota(jnp.int32, (width, width), 0)
    right = lax.broadcasted_iota(jnp.int32, (width, width), 1)
    perm = ((right % lb) * part + right // lb == left).astype(BF16)

    loads[0].wait()

    def turn(i, carry):
        f1t[i] = f1[i].T
        return carry

    lax.fori_loop(0, lb, turn, 0)
    loads[1].wait()

    def copy_to(sbuf, rbuf, ssem, rsem, c, peer):
        return pltpu.make_async_remote_copy(
            src_ref=sbuf.at[c, peer], dst_ref=rbuf.at[c, me], send_sem=ssem.at[c], recv_sem=rsem.at[c],
            device_id={"feat": peer}, device_id_type=pl.DeviceIdType.MESH)

    def send_all(sbuf, rbuf, ssem, rsem, c):
        def one(t, carry):
            copy_to(sbuf, rbuf, ssem, rsem, c, flip(me, n - 1 - t, n)).start()
            return carry

        lax.fori_loop(0, n - 1, one, 0)
        rbuf[c, me] = sbuf[c, me]

    def await_all(buf, sem, c):
        block = buf.at[c, pl.ds(0, n - 1)]
        pltpu.make_async_copy(block, block, sem.at[c]).wait()

    for c in range(chunks):
        col = jnp.broadcast_to(picks[pl.ds(c, 1), :].astype(F32), (CH, CH)).T.astype(jnp.int32)
        col = jnp.concatenate([col] * (patterns // CH), axis=1)
        pick = (col == lax.broadcasted_iota(jnp.int32, (CH, patterns), 1)).astype(BF16)

        def forward(p, carry):
            both = []
            for h in range(2):
                i = p * 2 + h
                cols = pl.ds(pl.multiple_of(i * width, width), width)
                x = dot(pick, arch[:, cols], 1, 0).astype(BF16)
                xc[i] = x
                y = dot(f1t[i], x, 1, 1)
                both.append(y.reshape(n, lb, CH))
            at = pl.ds(pl.multiple_of(p * 2 * lb, 2 * lb), 2 * lb)
            send[c, :, at, :] = jnp.concatenate(both, axis=1).astype(BF16)
            return carry

        lax.fori_loop(0, lb // 2, forward, 0)
        if c == 0:
            pl.semaphore_wait(barrier, n - 1)
        send_all(send, recv, send_sem, recv_sem, c)

        def turn_x(i, carry):
            xt[c, i] = xc[i].T
            return carry

        lax.fori_loop(0, lb, turn_x, 0)

    loads[2].wait()
    loads[3].wait()

    for c in range(chunks):
        await_all(recv, recv_sem, c)

        def permute(g, carry):
            four = recv[c, pl.ds(g * per, per)].reshape(width, CH)
            z = dot(perm, four, 1, 0).reshape(lb, part, CH)
            zbuf[:, pl.ds(pl.multiple_of(g * part, part), part), :] = z
            return carry

        lax.fori_loop(0, groups, permute, 0)

        def middle(j, carry):
            z = zbuf[j]
            sq = z * z
            t = jnp.tanh(ROOT * z * (1.0 + CUBE * sq))
            half = 0.5 * (1.0 + t)
            hidden = (z * half).astype(BF16)
            slope = half + 0.5 * z * (1.0 - t * t) * (ROOT * (1.0 + 3.0 * CUBE * sq))
            pred = dot(hidden, f2[j], 0, 0)
            cols = pl.ds(pl.multiple_of(j * width, width), width)
            want = goal[c * CH:(c + 1) * CH, cols].astype(F32)
            resid = ((pred - want) * scale).astype(BF16)
            grad = dot(hidden, resid, 1, 0)
            if c == 0:
                g2[j] = grad
            else:
                g2[j] += grad
            dh = dot(f2[j], resid, 1, 1)
            dzbuf[j] = (dh * slope).astype(BF16)
            return carry

        lax.fori_loop(0, lb, middle, 0)

        def back(g, carry):
            rows_in = dzbuf[:, pl.ds(pl.multiple_of(g * part, part), part), :].reshape(width, CH)
            out = dot(perm, rows_in, 0, 0).astype(BF16)
            bsend[c, pl.ds(g * per, per)] = out.reshape(per, cell, CH)
            return carry

        lax.fori_loop(0, groups, back, 0)
        send_all(bsend, brecv, bsend_sem, brecv_sem, c)

    out2 = pltpu.make_async_copy(g2, g2_hbm, out_sem.at[0])
    out2.start()

    for c in range(chunks):
        await_all(brecv, brecv_sem, c)

        def last(p, carry):
            at = pl.ds(pl.multiple_of(p * 2 * lb, 2 * lb), 2 * lb)
            both = brecv[c, :, at, :].astype(F32)
            for h in range(2):
                i = p * 2 + h
                d = both[:, h * lb:(h + 1) * lb, :].reshape(width, CH).astype(BF16)
                grad = dot(xt[c, i], d, 1, 1)
                if c == 0:
                    g1[i] = grad
                else:
                    g1[i] += grad
            return carry

        lax.fori_loop(0, lb // 2, last, 0)

    out1 = pltpu.make_async_copy(g1, g1_hbm, out_sem.at[1])
    out1.start()
    for c in range(chunks):
        await_all(send, send_sem, c)
        await_all(bsend, bsend_sem, c)
    out2.wait()
    out1.wait()


def fused(n, archive, picks, first_factor, second_factor, targets, scale):
    rows = picks.shape[0]
    lb, width, _ = first_factor.shape
    chunks = rows // CH
    any_ = pl.BlockSpec(memory_space=pl.ANY)
    grads = jax.ShapeDtypeStruct((lb, width, width), F32)
    block = pltpu.VMEM((chunks, n, lb * lb, CH), BF16)
    dma = pltpu.SemaphoreType.DMA
    return pl.pallas_call(
        functools.partial(kernel, n, lb, scale),
        out_shape=(grads, grads),
        in_specs=[pl.BlockSpec(memory_space=pltpu.VMEM)] + [any_] * 4,
        out_specs=(any_, any_),
        scratch_shapes=[
            pltpu.VMEM(archive.shape, BF16),
            pltpu.VMEM(first_factor.shape, BF16),
            pltpu.VMEM(second_factor.shape, BF16),
            pltpu.VMEM(targets.shape, BF16),
            pltpu.VMEM(first_factor.shape, BF16),
            pltpu.VMEM((lb, CH, width), BF16),
            pltpu.VMEM((chunks, lb, width, CH), BF16),
            block, block, block, block,
            pltpu.VMEM((lb, width, CH), F32),
            pltpu.VMEM((lb, width, CH), BF16),
            pltpu.VMEM((lb, width, width), F32),
            pltpu.VMEM((lb, width, width), F32),
            dma((4,)), dma((2,)),
            dma((chunks,)), dma((chunks,)), dma((chunks,)), dma((chunks,)),
        ],
        compiler_params=pltpu.CompilerParams(
            collective_id=0, has_side_effects=True, vmem_limit_bytes=48 * 1024 * 1024),
        cost_estimate=pl.CostEstimate(flops=10 * rows * lb * width * width, bytes_accessed=16 * 2**20, transcendentals=0),
    )(picks.reshape(chunks, CH), archive, first_factor, second_factor, targets)


def plain(archive, picks, first_factor, second_factor, targets, scale):
    rows = picks.shape[0]
    local_blocks = first_factor.shape[0]
    width = first_factor.shape[1]
    x = jnp.take(archive, picks, axis=0).reshape(rows, local_blocks, width)
    y_first = jnp.einsum("sia,iab->ibs", x, first_factor, preferred_element_type=F32).astype(BF16)
    z = lax.all_to_all(y_first, "feat", split_axis=1, concat_axis=0, tiled=True)
    z_float = z.astype(F32)
    hidden = jax.nn.gelu(z_float).astype(BF16)
    pred = jnp.einsum("ijs,jik->sjk", hidden, second_factor, preferred_element_type=F32)
    goal = targets.reshape(rows, local_blocks, width).astype(F32)
    resid = ((pred - goal) * scale).astype(BF16)
    grad_two = jnp.einsum("ijs,sjk->jik", hidden, resid, preferred_element_type=F32)
    d_hidden = jnp.einsum("sjk,jik->ijs", resid, second_factor, preferred_element_type=F32)
    d_z = jax.vjp(jax.nn.gelu, z_float)[1](d_hidden)[0].astype(BF16)
    d_first = lax.all_to_all(d_z, "feat", split_axis=0, concat_axis=1, tiled=True)
    grad_one = jnp.einsum("sia,ibs->iab", x, d_first, preferred_element_type=F32)
    return grad_one, grad_two


def local(archive, picks, first_factor, second_factor, targets):
    rows = picks.shape[0]
    lb, width, _ = first_factor.shape
    n = lax.axis_size("feat")
    dp = lax.axis_size("dp")
    scale = 1.0 / math.sqrt(rows * dp)
    args = (archive, picks, first_factor, second_factor, targets)
    fits = (lb == 8 and n * lb == width and width == 256 and n == 32 and rows % CH == 0
            and archive.shape[0] % CH == 0 and archive.shape[0] <= 1024 and rows <= 512)
    if fits:
        grad_one, grad_two = fused(n, *args, scale)
    else:
        grad_one, grad_two = plain(*args, scale)
    if dp > 1:
        half = width // dp
        offset = lax.axis_index("dp") * half
        one, two = lax.psum((grad_one.astype(BF16), grad_two.astype(BF16)), "dp")
        grad_one = lax.dynamic_slice_in_dim(one.astype(F32), offset, half, 1)
        grad_two = lax.dynamic_slice_in_dim(two.astype(F32), offset, half, 1)
    return grad_one, grad_two


def solution(mesh):
    return jax.shard_map(
        local,
        mesh=mesh,
        in_specs=(
            P("grp", "feat"),
            P(("grp", "dp")),
            P(("grp", "feat"), None, None),
            P(("grp", "feat"), None, None),
            P(("grp", "dp"), "feat"),
        ),
        out_specs=(P(("grp", "feat"), "dp", None), P(("grp", "feat"), "dp", None)),
        check_vma=False,
    )
```

time: 153 us -> 110 us (0.72)
  Pallas kernels: 0 us -> 102 us
  waiting for transfers between devices: 83.7 us -> 0 us
  local copies, waits for them, and re-layouts: 33.2 us -> 6.78 us
  matrix products: 20.9 us -> 0 us
  starting transfers between devices: 11.4 us -> 0 us
  other arithmetic: 2.15 us -> 0 us
    pallas_call x0 -> x1, Pallas kernels: none -> 102 us  [fused(): pl.pallas_call(functools.partial(kernel, n, lb, scale), out_shape=(grads,...]
    all_to_all x2 -> x0, waiting for transfers between devices: 83.7 us -> none  [the longest x1 42.9 us: local(): lax.all_to_all(d_z, 'feat', split_axis=0, concat_axis=1, tiled=True)]
    dot_general x5 -> x0, matrix products: 20.9 us -> none  [the longest x1 6.01 us: local(): jnp.einsum('ijs,sjk->jik', hidden, resid, preferred_element_type=jnp.floa...]
    convert_element_type x5 -> x0, local copies, waits for them, and re-layouts: 18.2 us -> none  [the longest x2 7.86 us: local(): z_float = z.astype(jnp.float32)]
    all_to_all x2 -> x0, starting transfers between devices: 11.4 us -> none  [the longest x1 7.3 us: local(): z = lax.all_to_all(y_first, 'feat', split_axis=1, concat_axis=0, tiled=True)]
    gather x2 -> x0, local copies, waits for them, and re-layouts: 9.64 us -> none  [local(): x = jnp.take(archive, picks, axis=0).reshape(rows, local_blocks, width)]
    unnamed x9 -> x10, local copies, waits for them, and re-layouts: 5.3 us -> 6.78 us
  transfers between devices with their start and end apart: 2 -> 0, of which waited for: 2 -> 0; matrix products, arithmetic and copies ran while one was open for 9% -> 0% of each run, Pallas kernels for 0% -> 0%
where the time goes in v1:
time: 110 us
  Pallas kernels  102 us (93%)
  local copies, waits for them, and re-layouts  6.78 us (6%)
    pallas_call x1, Pallas kernels, fused(): pl.pallas_call(functools.partial(kernel, n, lb, scale), out_shape=(grads,...  102 us
    unnamed x10, local copies, waits for them, and re-layouts  6.78 us

profile of v1, /device:TPU:0, one launch (start us, length us, event | category | flops | bytes accessed | tf_op | source)
XLA Modules:
  0.0 109.8 jit_solution(12728889579314149877)
XLA Ops:
  0.6 0.0 copy-start
  0.6 1.2 %copy-done = bf16[8,256,256]{2,1,0:T(8,128)(2,1)S(1)} copy-done((bf16[8,256,256]{2,1,0:T(8,128)(2,1)S(1)}, bf16[8,256,256]{2,1,0:T(8,128)(2,1)}, u32[]{:S(2)}) %copy-start) | copy-done | bytes 1048600
  1.9 0.0 copy-start.1
  1.9 1.2 %copy-done.1 = bf16[8,256,256]{2,1,0:T(8,128)(2,1)S(1)} copy-done((bf16[8,256,256]{2,1,0:T(8,128)(2,1)S(1)}, bf16[8,256,256]{2,1,0:T(8,128)(2,1)}, u32[]{:S(2)}) %copy-start.1) | copy-done | bytes 1048600
  3.1 0.0 copy-start.2
  3.1 0.7 copy-done.2
  3.8 102.3 %shard_map.68 = (f32[8,256,256]{2,1,0:T(8,128)S(1)}, f32[8,256,256]{2,1,0:T(8,128)}) custom-call(s32[4,128]{1,0:T(4,128)S(1)} %bitcast.1, bf16[1024,2048]{1,0:T(8,128)(2,1)} %arch_hbm.1, bf16[8,256,256]{2,1,0:T(8,128)(2,1)S(1)} %copy-done, bf16[8,256,256]{2,1,0:T(8,128)(2,1)S(1)} %copy-done.1, bf16[512,2048]{1,0:T(8,128)(2,1)} %goal_hbm.1), custom_call_target="tpu_custom_call" | custom-call | flops 2684354560 | bytes 16777216 | tf_op jit(solution)/shard_map/pallas_call | solution.py:201
  106.1 0.0 copy-start.3
  106.1 1.3 %copy.9 = f32[8,256,256]{2,1,0:T(8,128)} copy(f32[8,256,256]{2,1,0:T(8,128)S(1)} %get-tuple-element.4) | data formatting | bytes 4194304
  107.4 1.0 copy-done.3
  108.4 1.3 %copy.10 = f32[8,256,256]{2,1,0:T(8,128)} copy(f32[8,256,256]{2,1,0:T(8,128)S(1)} %copy-done.3) | data formatting | bytes 4194304
Async XLA Ops:
  0.6 1.2 %copy-start = (bf16[8,256,256]{2,1,0:T(8,128)(2,1)S(1)}, bf16[8,256,256]{2,1,0:T(8,128)(2,1)}, u32[]{:S(2)}) copy-start(bf16[8,256,256]{2,1,0:T(8,128)(2,1)} %f1_hbm.1) | copy-start | bytes 3145732
  1.9 1.2 %copy-start.1 = (bf16[8,256,256]{2,1,0:T(8,128)(2,1)S(1)}, bf16[8,256,256]{2,1,0:T(8,128)(2,1)}, u32[]{:S(2)}) copy-start(bf16[8,256,256]{2,1,0:T(8,128)(2,1)} %f2_hbm.1) | copy-start | bytes 3145732
  3.1 0.7 copy-start.2
  106.1 2.3 %copy-start.3 = (f32[8,256,256]{2,1,0:T(8,128)S(1)}, f32[8,256,256]{2,1,0:T(8,128)}, u32[]{:S(2)}) copy-start(f32[8,256,256]{2,1,0:T(8,128)} %get-tuple-element.5) | copy-start | bytes 6291460

commit v2 on v1

--- a/solution.py
+++ b/solution.py
@@ -11,6 +11,7 @@
 BF16 = jnp.bfloat16
 F32 = jnp.float32
 CH = 128
+FOLDS = (4, 1)
 ROOT = math.sqrt(2.0 / math.pi)
 CUBE = 0.044715
 
@@ -28,17 +29,47 @@
     return out
 
 
-def kernel(n, lb, scale, picks, arch_hbm, f1_hbm, f2_hbm, goal_hbm, g1_hbm, g2_hbm,
-           arch, f1, f2, goal, f1t, xc, xt, send, recv, bsend, brecv, zbuf, dzbuf, g1, g2,
+def ranker(picks, place, count):
+    chunks = picks.shape[0]
+    blocks = place.shape[0]
+    lane = lax.broadcasted_iota(jnp.int32, (CH, CH), 1)
+    sub = lax.broadcasted_iota(jnp.int32, (CH, CH), 0)
+    hits = [jnp.zeros((8, CH), F32) for _ in range(blocks)]
+    for c in range(chunks):
+        col = jnp.broadcast_to(picks[pl.ds(c, 1), :].astype(F32), (CH, CH)).T.astype(jnp.int32)
+        for b in range(blocks):
+            hit = (col == lane + b * CH).astype(F32)
+            hits[b] = jnp.maximum(hits[b], jnp.max(hit.reshape(CH // 8, 8, CH), axis=0))
+    seen = jnp.concatenate([jnp.max(h, axis=0, keepdims=True) for h in hits], axis=0)
+    seen_b = seen.astype(BF16)
+    before = dot(seen_b, (sub < lane).astype(BF16), 1, 0)
+    rows = lax.broadcasted_iota(jnp.int32, (blocks, blocks), 0)
+    cols = lax.broadcasted_iota(jnp.int32, (blocks, blocks), 1)
+    above = jnp.sum(dot((cols < rows).astype(BF16), seen_b, 1, 0), axis=1, keepdims=True)
+    place[...] = jnp.where(seen > 0.5, before + above, -1.0).astype(jnp.int32)
+    count[0, 0] = jnp.sum(seen).astype(jnp.int32)
+
+
+def rank(picks, patterns):
+    return pl.pallas_call(
+        ranker,
+        out_shape=(jax.ShapeDtypeStruct((patterns // CH, CH), jnp.int32), jax.ShapeDtypeStruct((1, 1), jnp.int32)),
+        in_specs=[pl.BlockSpec(memory_space=pltpu.VMEM)],
+        out_specs=(pl.BlockSpec(memory_space=pltpu.VMEM), pl.BlockSpec(memory_space=pltpu.SMEM)),
+    )(picks)
+
+
+def kernel(n, lb, folds, scale, picks, place, arch_hbm, f1_hbm, f2_hbm, goal_hbm, g1_hbm, g2_hbm,
+           arch, f1, f2, goal, f1t, xc, xt, send, recv, bsend, brecv, zbuf, dzbuf, g1, g2, hot, pick_keep,
            in_sem, out_sem, send_sem, recv_sem, bsend_sem, brecv_sem):
     me = lax.axis_index("feat")
     width = n * lb
     rows = goal.shape[0]
-    chunks = rows // CH
+    chunks = len(folds)
     patterns = arch.shape[0]
+    blocks = patterns // CH
     cell = lb * lb
     per = width // cell
-    groups = n // per
     part = per * lb
 
     loads = [
@@ -60,6 +91,18 @@
     right = lax.broadcasted_iota(jnp.int32, (width, width), 1)
     perm = ((right % lb) * part + right // lb == left).astype(BF16)
 
+    def fold_matrix(fold):
+        few = lb // fold
+        i = right % lb
+        return ((i // few) * (n * few) + (right // lb) * few + i % few == left).astype(BF16)
+
+    def chosen(c, q):
+        span = CH // folds[c]
+        row = lax.broadcasted_iota(jnp.int32, (CH, CH), 0) - q * span
+        slot = jnp.where((row >= 0) & (row < span), row + c * CH, -2)
+        return jnp.concatenate(
+            [(place[pl.ds(b, 1), :] == slot).astype(BF16) for b in range(blocks)], axis=1)
+
     loads[0].wait()
 
     def turn(i, carry):
@@ -69,9 +112,13 @@
     lax.fori_loop(0, lb, turn, 0)
     loads[1].wait()
 
+    def cells(c):
+        return pl.ds(0, cell // folds[c])
+
     def copy_to(sbuf, rbuf, ssem, rsem, c, peer):
         return pltpu.make_async_remote_copy(
-            src_ref=sbuf.at[c, peer], dst_ref=rbuf.at[c, me], send_sem=ssem.at[c], recv_sem=rsem.at[c],
+            src_ref=sbuf.at[c, peer, cells(c)], dst_ref=rbuf.at[c, me, cells(c)],
+            send_sem=ssem.at[c], recv_sem=rsem.at[c],
             device_id={"feat": peer}, device_id_type=pl.DeviceIdType.MESH)
 
     def send_all(sbuf, rbuf, ssem, rsem, c):
@@ -80,31 +127,35 @@
             return carry
 
         lax.fori_loop(0, n - 1, one, 0)
-        rbuf[c, me] = sbuf[c, me]
+        rbuf[c, me, cells(c)] = sbuf[c, me, cells(c)]
 
     def await_all(buf, sem, c):
-        block = buf.at[c, pl.ds(0, n - 1)]
+        block = buf.at[c, pl.ds(0, n - 1), cells(c)]
         pltpu.make_async_copy(block, block, sem.at[c]).wait()
 
     for c in range(chunks):
-        col = jnp.broadcast_to(picks[pl.ds(c, 1), :].astype(F32), (CH, CH)).T.astype(jnp.int32)
-        col = jnp.concatenate([col] * (patterns // CH), axis=1)
-        pick = (col == lax.broadcasted_iota(jnp.int32, (CH, patterns), 1)).astype(BF16)
+        fold = folds[c]
+        few = lb // fold
+        for q in range(fold):
+            pick_keep[q] = chosen(c, q)
 
         def forward(p, carry):
             both = []
             for h in range(2):
-                i = p * 2 + h
-                cols = pl.ds(pl.multiple_of(i * width, width), width)
-                x = dot(pick, arch[:, cols], 1, 0).astype(BF16)
-                xc[i] = x
-                y = dot(f1t[i], x, 1, 1)
+                y = None
+                for q in range(fold):
+                    i = q * few + p * 2 + h
+                    cols = pl.ds(pl.multiple_of(i * width, width), width)
+                    x = dot(pick_keep[q], arch[:, cols], 1, 0).astype(BF16)
+                    xc[i] = x
+                    term = dot(f1t[i], x, 1, 1)
+                    y = term if y is None else y + term
                 both.append(y.reshape(n, lb, CH))
             at = pl.ds(pl.multiple_of(p * 2 * lb, 2 * lb), 2 * lb)
             send[c, :, at, :] = jnp.concatenate(both, axis=1).astype(BF16)
             return carry
 
-        lax.fori_loop(0, lb // 2, forward, 0)
+        lax.fori_loop(0, few // 2, forward, 0)
         if c == 0:
             pl.semaphore_wait(barrier, n - 1)
         send_all(send, recv, send_sem, recv_sem, c)
@@ -115,22 +166,40 @@
 
         lax.fori_loop(0, lb, turn_x, 0)
 
+    for c in range(rows // CH):
+        col = jnp.broadcast_to(picks[pl.ds(c, 1), :].astype(F32), (CH, CH)).T.astype(jnp.int32)
+        lane = lax.broadcasted_iota(jnp.int32, (CH, CH), 1)
+        for b in range(blocks):
+            hot[c * CH:(c + 1) * CH, b * CH:(b + 1) * CH] = (col == lane + b * CH).astype(BF16)
+
     loads[2].wait()
     loads[3].wait()
 
     for c in range(chunks):
+        fold = folds[c]
+        span = CH // fold
+        tall = width // fold
+        member = dot(chosen(c, 0), hot[...], 1, 1)
+        times = jnp.sum(member, axis=1, keepdims=True)
+        member = member.astype(BF16)
+        many = per * fold
         await_all(recv, recv_sem, c)
 
         def permute(g, carry):
-            four = recv[c, pl.ds(g * per, per)].reshape(width, CH)
-            z = dot(perm, four, 1, 0).reshape(lb, part, CH)
+            got = recv[c, pl.ds(g * many, many), cells(c)].reshape(width, CH)
+            z = dot(perm, got, 1, 0).reshape(lb, part, CH)
             zbuf[:, pl.ds(pl.multiple_of(g * part, part), part), :] = z
             return carry
 
-        lax.fori_loop(0, groups, permute, 0)
+        lax.fori_loop(0, n // many, permute, 0)
 
         def middle(j, carry):
-            z = zbuf[j]
+            if fold == 1:
+                z = zbuf[j]
+            else:
+                flat = zbuf[j, pl.ds(0, tall), :]
+                pieces = [flat if q == 0 else pltpu.roll(flat, CH - q * span, 1) for q in range(fold)]
+                z = dot(fold_matrix(fold), jnp.concatenate(pieces, axis=0).astype(BF16), 0, 0)
             sq = z * z
             t = jnp.tanh(ROOT * z * (1.0 + CUBE * sq))
             half = 0.5 * (1.0 + t)
@@ -138,15 +207,23 @@
             slope = half + 0.5 * z * (1.0 - t * t) * (ROOT * (1.0 + 3.0 * CUBE * sq))
             pred = dot(hidden, f2[j], 0, 0)
             cols = pl.ds(pl.multiple_of(j * width, width), width)
-            want = goal[c * CH:(c + 1) * CH, cols].astype(F32)
-            resid = ((pred - want) * scale).astype(BF16)
+            want = dot(member, goal[:, cols], 1, 0)
+            resid = ((times * pred - want) * scale).astype(BF16)
             grad = dot(hidden, resid, 1, 0)
             if c == 0:
                 g2[j] = grad
             else:
                 g2[j] += grad
             dh = dot(f2[j], resid, 1, 1)
-            dzbuf[j] = (dh * slope).astype(BF16)
+            dz = (dh * slope).astype(BF16)
+            if fold == 1:
+                dzbuf[j] = dz
+            else:
+                flat = dot(fold_matrix(fold), dz, 1, 0)
+                total = flat[:tall]
+                for q in range(1, fold):
+                    total = total + pltpu.roll(flat[q * tall:(q + 1) * tall], q * span, 1)
+                dzbuf[j, pl.ds(0, tall), :] = total.astype(BF16)
             return carry
 
         lax.fori_loop(0, lb, middle, 0)
@@ -154,32 +231,35 @@
         def back(g, carry):
             rows_in = dzbuf[:, pl.ds(pl.multiple_of(g * part, part), part), :].reshape(width, CH)
             out = dot(perm, rows_in, 0, 0).astype(BF16)
-            bsend[c, pl.ds(g * per, per)] = out.reshape(per, cell, CH)
-            return carry
-
-        lax.fori_loop(0, groups, back, 0)
+            bsend[c, pl.ds(g * many, many), cells(c)] = out.reshape(many, cell // fold, CH)
+            return carry
+
+        lax.fori_loop(0, n // many, back, 0)
         send_all(bsend, brecv, bsend_sem, brecv_sem, c)
 
     out2 = pltpu.make_async_copy(g2, g2_hbm, out_sem.at[0])
     out2.start()
 
     for c in range(chunks):
+        fold = folds[c]
+        few = lb // fold
         await_all(brecv, brecv_sem, c)
 
         def last(p, carry):
             at = pl.ds(pl.multiple_of(p * 2 * lb, 2 * lb), 2 * lb)
             both = brecv[c, :, at, :].astype(F32)
             for h in range(2):
-                i = p * 2 + h
                 d = both[:, h * lb:(h + 1) * lb, :].reshape(width, CH).astype(BF16)
-                grad = dot(xt[c, i], d, 1, 1)
-                if c == 0:
-                    g1[i] = grad
-                else:
-                    g1[i] += grad
-            return carry
-
-        lax.fori_loop(0, lb // 2, last, 0)
+                for q in range(fold):
+                    i = q * few + p * 2 + h
+                    grad = dot(xt[c, i], d, 1, 1)
+                    if c == 0:
+                        g1[i] = grad
+                    else:
+                        g1[i] += grad
+            return carry
+
+        lax.fori_loop(0, few // 2, last, 0)
 
     out1 = pltpu.make_async_copy(g1, g1_hbm, out_sem.at[1])
     out1.start()
@@ -190,18 +270,18 @@
     out1.wait()
 
 
-def fused(n, archive, picks, first_factor, second_factor, targets, scale):
-    rows = picks.shape[0]
+def fused(n, scale, which, folds, picks, place, archive, first_factor, second_factor, targets):
+    rows = targets.shape[0]
     lb, width, _ = first_factor.shape
-    chunks = rows // CH
+    chunks = len(folds)
     any_ = pl.BlockSpec(memory_space=pl.ANY)
     grads = jax.ShapeDtypeStruct((lb, width, width), F32)
     block = pltpu.VMEM((chunks, n, lb * lb, CH), BF16)
     dma = pltpu.SemaphoreType.DMA
     return pl.pallas_call(
-        functools.partial(kernel, n, lb, scale),
+        functools.partial(kernel, n, lb, folds, scale),
         out_shape=(grads, grads),
-        in_specs=[pl.BlockSpec(memory_space=pltpu.VMEM)] + [any_] * 4,
+        in_specs=[pl.BlockSpec(memory_space=pltpu.VMEM)] * 2 + [any_] * 4,
         out_specs=(any_, any_),
         scratch_shapes=[
             pltpu.VMEM(archive.shape, BF16),
@@ -216,13 +296,30 @@
             pltpu.VMEM((lb, width, CH), BF16),
             pltpu.VMEM((lb, width, width), F32),
             pltpu.VMEM((lb, width, width), F32),
+            pltpu.VMEM((rows, archive.shape[0]), BF16),
+            pltpu.VMEM((max(folds), CH, archive.shape[0]), BF16),
             dma((4,)), dma((2,)),
             dma((chunks,)), dma((chunks,)), dma((chunks,)), dma((chunks,)),
         ],
         compiler_params=pltpu.CompilerParams(
-            collective_id=0, has_side_effects=True, vmem_limit_bytes=48 * 1024 * 1024),
+            collective_id=which, has_side_effects=True, vmem_limit_bytes=60 * 1024 * 1024),
         cost_estimate=pl.CostEstimate(flops=10 * rows * lb * width * width, bytes_accessed=16 * 2**20, transcendentals=0),
-    )(picks.reshape(chunks, CH), archive, first_factor, second_factor, targets)
+    )(picks, place, archive, first_factor, second_factor, targets)
+
+
+def distinct(n, scale, archive, picks, first_factor, second_factor, targets):
+    chunks = picks.shape[0] // CH
+    picks = picks.reshape(chunks, CH)
+    place, count = rank(picks, archive.shape[0])
+    count = count[0, 0]
+    if lax.axis_size("grp") * lax.axis_size("dp") > 1:
+        count = lax.pmax(count, ("grp", "dp"))
+    plans = [(1,) * (chunks - 1) + (fold,) for fold in FOLDS]
+    index = 0
+    for folds in plans[:-1]:
+        index = index + (count > sum(CH // fold for fold in folds)).astype(jnp.int32)
+    calls = [functools.partial(fused, n, scale, which, folds) for which, folds in enumerate(plans)]
+    return lax.switch(index, calls, picks, place, archive, first_factor, second_factor, targets)
 
 
 def plain(archive, picks, first_factor, second_factor, targets, scale):
@@ -255,7 +352,7 @@
     fits = (lb == 8 and n * lb == width and width == 256 and n == 32 and rows % CH == 0
             and archive.shape[0] % CH == 0 and archive.shape[0] <= 1024 and rows <= 512)
     if fits:
-        grad_one, grad_two = fused(n, *args, scale)
+        grad_one, grad_two = distinct(n, scale, *args)
     else:
         grad_one, grad_two = plain(*args, scale)
     if dp > 1:

time: 110 us -> 93.7 us (0.85)
  Pallas kernels: 102 us -> 88.4 us
  local copies, waits for them, and re-layouts: 6.78 us -> 3.66 us
    pallas_call x1 -> x2, Pallas kernels: 102 us -> 88.4 us  [the longest x1 86.7 us: fused(): pl.pallas_call(functools.partial(kernel, n, lb, folds, scale), out_shape=...]
    unnamed x10 -> x4, local copies, waits for them, and re-layouts: 6.78 us -> 3.66 us
where the time goes in v2:
time: 93.7 us; the launch traced here: 93.5 us
  Pallas kernels  88.4 us (94%)
  local copies, waits for them, and re-layouts  3.66 us (4%)
  between operations  1.31 us (1%)
    pallas_call x1, Pallas kernels, fused(): pl.pallas_call(functools.partial(kernel, n, lb, folds, scale), out_shape=...  86.7 us
    unnamed x4, local copies, waits for them, and re-layouts  3.66 us

profile of v2, /device:TPU:0, one launch (start us, length us, event | category | flops | bytes accessed | tf_op | source)
XLA Modules:
  0.0 93.5 jit_solution(14126156003158895722)
XLA Ops:
  0.6 1.7 %shard_map.72 = (s32[8,128]{1,0:T(8,128)S(1)}, s32[1,1]{1,0:T(1,128)}) custom-call(s32[4,128]{1,0:T(4,128)} %bitcast.2), custom_call_target="tpu_custom_call" | custom-call | tf_op jit(solution)/shard_map/pallas_call | solution.py:54
  3.0 86.9 %conditional.1 = ((f32[8,256,256]{2,1,0:T(8,128)S(1)}, f32[8,256,256]{2,1,0:T(8,128)})) conditional(s32[]{:T(128)} %bitcast.1, (s32[4,128]{1,0:T(4,128)}, s32[8,128]{1,0:T(8,128)S(1)}, bf16[1024,2048]{1,0:T(8,128)(2,1)}, bf16[8,256,256]{2,1,0:T(8,128)(2,1)}, bf16[8,256,256]{2,1,0:T(8,128)(2,1)}, /*index=5*/bf16[512,2048]{1,0:T(8,128)(2,1)}) %tuple.24, ...), branch_computations={%region_0.0_spmd, %region_1.0_spmd} | conditional | flops 2684354560 | bytes 16777224 | solution.py:322
  3.0 86.7 %branch_0_fun.1 = (f32[8,256,256]{2,1,0:T(8,128)S(1)}, f32[8,256,256]{2,1,0:T(8,128)}) custom-call(s32[4,128]{1,0:T(4,128)} %get-tuple-element.24.picks, s32[8,128]{1,0:T(8,128)S(1)} %get-tuple-element.25.place, bf16[1024,2048]{1,0:T(8,128)(2,1)} %get-tuple-element.26.arch_hbm, bf16[8,256,256]{2,1,0:T(8,128)(2,1)} %get-tuple-element.27.f1_hbm, ...), custom_call_target="tpu_custom_call" | custom-call | flops 2684354560 | bytes 16777216 | tf_op jit(solution)/shard_map/cond/branch_0_fun/pallas_call | solution.py:281
  89.9 0.0 copy-start
  89.9 1.3 %copy.17 = f32[8,256,256]{2,1,0:T(8,128)} copy(f32[8,256,256]{2,1,0:T(8,128)S(1)} %get-tuple-element.54) | data formatting | bytes 4194304
  91.2 1.0 %copy-done = f32[8,256,256]{2,1,0:T(8,128)S(1)} copy-done((f32[8,256,256]{2,1,0:T(8,128)S(1)}, f32[8,256,256]{2,1,0:T(8,128)}, u32[]{:S(2)}) %copy-start) | copy-done | bytes 2097176
  92.2 1.3 %copy.18 = f32[8,256,256]{2,1,0:T(8,128)} copy(f32[8,256,256]{2,1,0:T(8,128)S(1)} %copy-done) | data formatting | bytes 4194304
Async XLA Ops:
  89.9 2.3 %copy-start = (f32[8,256,256]{2,1,0:T(8,128)S(1)}, f32[8,256,256]{2,1,0:T(8,128)}, u32[]{:S(2)}) copy-start(f32[8,256,256]{2,1,0:T(8,128)} %get-tuple-element.55) | copy-start | bytes 6291460

commit v3 on v2

--- a/solution.py
+++ b/solution.py
@@ -60,8 +60,8 @@
 
 
 def kernel(n, lb, folds, scale, picks, place, arch_hbm, f1_hbm, f2_hbm, goal_hbm, g1_hbm, g2_hbm,
-           arch, f1, f2, goal, f1t, xc, xt, send, recv, bsend, brecv, zbuf, dzbuf, g1, g2, hot, pick_keep,
-           in_sem, out_sem, send_sem, recv_sem, bsend_sem, brecv_sem):
+           arch, f1, f2, goal, f1t, xc, xt, send, recv, bsend, brecv, zbuf, dzbuf, g1, g2, g1b, g2b, hot, pick_keep,
+           in_sem, f1_sem, arch_sem, out_sem, send_sem, recv_sem, bsend_sem, brecv_sem):
     me = lax.axis_index("feat")
     width = n * lb
     rows = goal.shape[0]
@@ -72,10 +72,19 @@
     per = width // cell
     part = per * lb
 
+    def load_pair(p):
+        some = pl.ds(p * 2, 2)
+        cols = pl.ds(pl.multiple_of(p * 2 * width, 2 * width), 2 * width)
+        return (pltpu.make_async_copy(f1_hbm.at[some], f1.at[some], f1_sem.at[p]),
+                pltpu.make_async_copy(arch_hbm.at[:, cols], arch.at[:, cols], arch_sem.at[p]))
+
     loads = [
         pltpu.make_async_copy(src, dst, in_sem.at[t])
-        for t, (src, dst) in enumerate(((f1_hbm, f1), (arch_hbm, arch), (f2_hbm, f2), (goal_hbm, goal)))
+        for t, (src, dst) in enumerate(((f2_hbm, f2), (goal_hbm, goal)))
     ]
+    for p in range(lb // 2):
+        for load in load_pair(p):
+            load.start()
     for load in loads:
         load.start()
 
@@ -103,31 +112,23 @@
         return jnp.concatenate(
             [(place[pl.ds(b, 1), :] == slot).astype(BF16) for b in range(blocks)], axis=1)
 
-    loads[0].wait()
-
-    def turn(i, carry):
-        f1t[i] = f1[i].T
-        return carry
-
-    lax.fori_loop(0, lb, turn, 0)
-    loads[1].wait()
-
     def cells(c):
         return pl.ds(0, cell // folds[c])
 
-    def copy_to(sbuf, rbuf, ssem, rsem, c, peer):
+    def copy_to(sbuf, rbuf, ssem, rsem, c, peer, at):
         return pltpu.make_async_remote_copy(
-            src_ref=sbuf.at[c, peer, cells(c)], dst_ref=rbuf.at[c, me, cells(c)],
+            src_ref=sbuf.at[c, peer, at], dst_ref=rbuf.at[c, me, at],
             send_sem=ssem.at[c], recv_sem=rsem.at[c],
             device_id={"feat": peer}, device_id_type=pl.DeviceIdType.MESH)
 
-    def send_all(sbuf, rbuf, ssem, rsem, c):
+    def send_all(sbuf, rbuf, ssem, rsem, c, at):
         def one(t, carry):
-            copy_to(sbuf, rbuf, ssem, rsem, c, flip(me, n - 1 - t, n)).start()
+            peer = flip(me, n - 1 - t // 2 - (t % 2) * (n // 2), n)
+            copy_to(sbuf, rbuf, ssem, rsem, c, peer, at).start()
             return carry
 
         lax.fori_loop(0, n - 1, one, 0)
-        rbuf[c, me, cells(c)] = sbuf[c, me, cells(c)]
+        rbuf[c, me, at] = sbuf[c, me, at]
 
     def await_all(buf, sem, c):
         block = buf.at[c, pl.ds(0, n - 1), cells(c)]
@@ -141,6 +142,11 @@
 
         def forward(p, carry):
             both = []
+            if c == 0:
+                for load in load_pair(p):
+                    load.wait()
+                for h in range(2):
+                    f1t[p * 2 + h] = f1[p * 2 + h].T
             for h in range(2):
                 y = None
                 for q in range(fold):
@@ -153,12 +159,15 @@
                 both.append(y.reshape(n, lb, CH))
             at = pl.ds(pl.multiple_of(p * 2 * lb, 2 * lb), 2 * lb)
             send[c, :, at, :] = jnp.concatenate(both, axis=1).astype(BF16)
-            return carry
-
-        lax.fori_loop(0, few // 2, forward, 0)
+            if c == 0:
+                send_all(send, recv, send_sem, recv_sem, c, at)
+            return carry
+
         if c == 0:
             pl.semaphore_wait(barrier, n - 1)
-        send_all(send, recv, send_sem, recv_sem, c)
+        lax.fori_loop(0, few // 2, forward, 0)
+        if c > 0:
+            send_all(send, recv, send_sem, recv_sem, c, cells(c))
 
         def turn_x(i, carry):
             xt[c, i] = xc[i].T
@@ -172,8 +181,8 @@
         for b in range(blocks):
             hot[c * CH:(c + 1) * CH, b * CH:(b + 1) * CH] = (col == lane + b * CH).astype(BF16)
 
-    loads[2].wait()
-    loads[3].wait()
+    loads[0].wait()
+    loads[1].wait()
 
     for c in range(chunks):
         fold = folds[c]
@@ -210,20 +219,21 @@
             want = dot(member, goal[:, cols], 1, 0)
             resid = ((times * pred - want) * scale).astype(BF16)
             grad = dot(hidden, resid, 1, 0)
-            if c == 0:
-                g2[j] = grad
+            total = grad if c == 0 else g2[j] + grad
+            if c < chunks - 1:
+                g2[j] = total
             else:
-                g2[j] += grad
+                g2b[j] = total.astype(BF16)
             dh = dot(f2[j], resid, 1, 1)
             dz = (dh * slope).astype(BF16)
             if fold == 1:
                 dzbuf[j] = dz
             else:
                 flat = dot(fold_matrix(fold), dz, 1, 0)
-                total = flat[:tall]
+                folded = flat[:tall]
                 for q in range(1, fold):
-                    total = total + pltpu.roll(flat[q * tall:(q + 1) * tall], q * span, 1)
-                dzbuf[j, pl.ds(0, tall), :] = total.astype(BF16)
+                    folded = folded + pltpu.roll(flat[q * tall:(q + 1) * tall], q * span, 1)
+                dzbuf[j, pl.ds(0, tall), :] = folded.astype(BF16)
             return carry
 
         lax.fori_loop(0, lb, middle, 0)
@@ -235,9 +245,9 @@
             return carry
 
         lax.fori_loop(0, n // many, back, 0)
-        send_all(bsend, brecv, bsend_sem, brecv_sem, c)
-
-    out2 = pltpu.make_async_copy(g2, g2_hbm, out_sem.at[0])
+        send_all(bsend, brecv, bsend_sem, brecv_sem, c, cells(c))
+
+    out2 = pltpu.make_async_copy(g2b, g2_hbm, out_sem.at[0])
     out2.start()
 
     for c in range(chunks):
@@ -253,15 +263,16 @@
                 for q in range(fold):
                     i = q * few + p * 2 + h
                     grad = dot(xt[c, i], d, 1, 1)
-                    if c == 0:
-                        g1[i] = grad
+                    total = grad if c == 0 else g1[i] + grad
+                    if c < chunks - 1:
+                        g1[i] = total
                     else:
-                        g1[i] += grad
+                        g1b[i] = total.astype(BF16)
             return carry
 
         lax.fori_loop(0, few // 2, last, 0)
 
-    out1 = pltpu.make_async_copy(g1, g1_hbm, out_sem.at[1])
+    out1 = pltpu.make_async_copy(g1b, g1_hbm, out_sem.at[1])
     out1.start()
     for c in range(chunks):
         await_all(send, send_sem, c)
@@ -275,7 +286,7 @@
     lb, width, _ = first_factor.shape
     chunks = len(folds)
     any_ = pl.BlockSpec(memory_space=pl.ANY)
-    grads = jax.ShapeDtypeStruct((lb, width, width), F32)
+    grads = jax.ShapeDtypeStruct((lb, width, width), BF16)
     block = pltpu.VMEM((chunks, n, lb * lb, CH), BF16)
     dma = pltpu.SemaphoreType.DMA
     return pl.pallas_call(
@@ -296,9 +307,11 @@
             pltpu.VMEM((lb, width, CH), BF16),
             pltpu.VMEM((lb, width, width), F32),
             pltpu.VMEM((lb, width, width), F32),
+            pltpu.VMEM(first_factor.shape, BF16),
+            pltpu.VMEM(first_factor.shape, BF16),
             pltpu.VMEM((rows, archive.shape[0]), BF16),
             pltpu.VMEM((max(folds), CH, archive.shape[0]), BF16),
-            dma((4,)), dma((2,)),
+            dma((2,)), dma((lb // 2,)), dma((lb // 2,)), dma((2,)),
             dma((chunks,)), dma((chunks,)), dma((chunks,)), dma((chunks,)),
         ],
         compiler_params=pltpu.CompilerParams(
@@ -319,7 +332,8 @@
     for folds in plans[:-1]:
         index = index + (count > sum(CH // fold for fold in folds)).astype(jnp.int32)
     calls = [functools.partial(fused, n, scale, which, folds) for which, folds in enumerate(plans)]
-    return lax.switch(index, calls, picks, place, archive, first_factor, second_factor, targets)
+    one, two = lax.switch(index, calls, picks, place, archive, first_factor, second_factor, targets)
+    return one.astype(F32), two.astype(F32)
 
 
 def plain(archive, picks, first_factor, second_factor, targets, scale):

time: 93.7 us -> 91.2 us (0.973)
  local copies, waits for them, and re-layouts: 3.66 us -> 0 us
  other arithmetic: 0 us -> 3.02 us
  Pallas kernels: 88.4 us -> 86.4 us
    unnamed x4 -> x0, local copies, waits for them, and re-layouts: 3.66 us -> none
    convert_element_type x0 -> x2, other arithmetic: none -> 3.02 us  [distinct(): return (one.astype(F32), two.astype(F32))]
    pallas_call x1, Pallas kernels: 86.7 us -> 84.7 us  [fused(): pl.pallas_call(functools.partial(kernel, n, lb, folds, scale), out_shape=...]
where the time goes in v3:
time: 91.2 us; the launch traced here: 90.9 us
  Pallas kernels  86.4 us (95%)
  other arithmetic  3.02 us (3%)
  between operations  1.3 us (1%)
    pallas_call x1, Pallas kernels, fused(): pl.pallas_call(functools.partial(kernel, n, lb, folds, scale), out_shape=...  84.7 us
    convert_element_type x2, other arithmetic, distinct(): return (one.astype(F32), two.astype(F32))  3.02 us

profile of v3, /device:TPU:0, one launch (start us, length us, event | category | flops | bytes accessed | tf_op | source)
XLA Modules:
  0.0 90.9 jit_solution(7823036036530489152)
XLA Ops:
  0.6 1.7 %shard_map.68 = (s32[8,128]{1,0:T(8,128)S(1)}, s32[1,1]{1,0:T(1,128)}) custom-call(s32[4,128]{1,0:T(4,128)} %bitcast.2), custom_call_target="tpu_custom_call" | custom-call | tf_op jit(solution)/shard_map/pallas_call | solution.py:54
  3.0 84.9 %conditional.4 = (bf16[8,256,256]{2,1,0:T(8,128)(2,1)S(1)}, bf16[8,256,256]{2,1,0:T(8,128)(2,1)S(1)}) conditional(s32[]{:T(128)} %bitcast.1, (s32[4,128]{1,0:T(4,128)}, s32[8,128]{1,0:T(8,128)S(1)}, bf16[1024,2048]{1,0:T(8,128)(2,1)}, bf16[8,256,256]{2,1,0:T(8,128)(2,1)}, bf16[8,256,256]{2,1,0:T(8,128)(2,1)}, ...), branch_computations={%region_0.0_spmd, %region_1.0_spmd} | conditional | flops 2684354560 | bytes 16777232
  3.0 84.7 %branch_0_fun.1 = (bf16[8,256,256]{2,1,0:T(8,128)(2,1)S(1)}, bf16[8,256,256]{2,1,0:T(8,128)(2,1)S(1)}) custom-call(s32[4,128]{1,0:T(4,128)} %get-tuple-element.44.picks, s32[8,128]{1,0:T(8,128)S(1)} %get-tuple-element.45.place, bf16[1024,2048]{1,0:T(8,128)(2,1)} %get-tuple-element.46.arch_hbm, bf16[8,256,256]{2,1,0:T(8,128)(2,1)} %get-tuple-element.47.f1_hbm, ...), custom_call_target="tpu_custom_call" | custom-call | flops 2684354560 | bytes 16777216 | tf_op jit(solution)/shard_map/cond/branch_0_fun/pallas_call | solution.py:292
  87.9 1.5 %convert_element_type.27 = f32[8,256,256]{2,1,0:T(8,128)} convert(bf16[8,256,256]{2,1,0:T(8,128)(2,1)S(1)} %get-tuple-element.73) | non-fusion elementwise | flops 524288 | bytes 3145728 | tf_op jit(solution)/shard_map/convert_element_type | solution.py:336
  89.4 1.5 %convert_element_type.24 = f32[8,256,256]{2,1,0:T(8,128)} convert(bf16[8,256,256]{2,1,0:T(8,128)(2,1)S(1)} %get-tuple-element.65) | non-fusion elementwise | flops 524288 | bytes 3145728 | tf_op jit(solution)/shard_map/convert_element_type | solution.py:336

commit v4 on v3

--- a/solution.py
+++ b/solution.py
@@ -123,7 +123,7 @@
 
     def send_all(sbuf, rbuf, ssem, rsem, c, at):
         def one(t, carry):
-            peer = flip(me, n - 1 - t // 2 - (t % 2) * (n // 2), n)
+            peer = flip(me, n - 1 - t, n)
             copy_to(sbuf, rbuf, ssem, rsem, c, peer, at).start()
             return carry
 
@@ -320,6 +320,20 @@
     )(picks, place, archive, first_factor, second_factor, targets)
 
 
+def widener(one, two, wide_one, wide_two):
+    wide_one[...] = one[...].astype(F32)
+    wide_two[...] = two[...].astype(F32)
+
+
+def widen(one, two):
+    lb, width, _ = one.shape
+    spec = pl.BlockSpec((2, width, width), lambda i: (i, 0, 0))
+    wide = jax.ShapeDtypeStruct(one.shape, F32)
+    return pl.pallas_call(
+        widener, grid=(lb // 2,), out_shape=(wide, wide), in_specs=[spec, spec], out_specs=(spec, spec),
+    )(one, two)
+
+
 def distinct(n, scale, archive, picks, first_factor, second_factor, targets):
     chunks = picks.shape[0] // CH
     picks = picks.reshape(chunks, CH)
@@ -333,7 +347,7 @@
         index = index + (count > sum(CH // fold for fold in folds)).astype(jnp.int32)
     calls = [functools.partial(fused, n, scale, which, folds) for which, folds in enumerate(plans)]
     one, two = lax.switch(index, calls, picks, place, archive, first_factor, second_factor, targets)
-    return one.astype(F32), two.astype(F32)
+    return widen(one, two)
 
 
 def plain(archive, picks, first_factor, second_factor, targets, scale):

time: 91.2 us -> 90 us (0.987)
  other arithmetic: 3.02 us -> 0 us
  Pallas kernels: 86.4 us -> 88.2 us
    convert_element_type x2 -> x0, other arithmetic: 3.02 us -> none  [distinct(): return (one.astype(F32), two.astype(F32))]
    pallas_call x0 -> x1, Pallas kernels: none -> 2.39 us  [widen(): pl.pallas_call(widener, grid=(lb // 2,), out_shape=(wide, wide), in_specs...]
where the time goes in v4:
time: 90 us; the launch traced here: 89.7 us
  Pallas kernels  88.2 us (98%)
  between operations  1.3 us (1%)
    pallas_call x1, Pallas kernels, fused(): pl.pallas_call(functools.partial(kernel, n, lb, folds, scale), out_shape=...  84.2 us
    pallas_call x1, Pallas kernels, widen(): pl.pallas_call(widener, grid=(lb // 2,), out_shape=(wide, wide), in_specs...  2.39 us

profile of v4, /device:TPU:0, one launch (start us, length us, event | category | flops | bytes accessed | tf_op | source)
XLA Modules:
  0.0 89.7 jit_solution(17436999803012817419)
XLA Ops:
  0.6 1.7 %shard_map.68 = (s32[8,128]{1,0:T(8,128)S(1)}, s32[1,1]{1,0:T(1,128)}) custom-call(s32[4,128]{1,0:T(4,128)} %bitcast.2), custom_call_target="tpu_custom_call" | custom-call | tf_op jit(solution)/shard_map/pallas_call | solution.py:54
  3.0 84.4 %conditional.1 = ((bf16[8,256,256]{2,1,0:T(8,128)(2,1)S(1)}, bf16[8,256,256]{2,1,0:T(8,128)(2,1)S(1)})) conditional(s32[]{:T(128)} %bitcast.1, (s32[4,128]{1,0:T(4,128)}, s32[8,128]{1,0:T(8,128)S(1)}, bf16[1024,2048]{1,0:T(8,128)(2,1)}, bf16[8,256,256]{2,1,0:T(8,128)(2,1)}, bf16[8,256,256]{2,1,0:T(8,128)(2,1)}, ...), branch_computations={%region_0.0_spmd, %region_1.0_spmd} | conditional | flops 2684354560 | bytes 16777224 | solution.py:349
  3.0 84.2 %branch_0_fun.1 = (bf16[8,256,256]{2,1,0:T(8,128)(2,1)S(1)}, bf16[8,256,256]{2,1,0:T(8,128)(2,1)S(1)}) custom-call(s32[4,128]{1,0:T(4,128)} %get-tuple-element.24.picks, s32[8,128]{1,0:T(8,128)S(1)} %get-tuple-element.25.place, bf16[1024,2048]{1,0:T(8,128)(2,1)} %get-tuple-element.26.arch_hbm, bf16[8,256,256]{2,1,0:T(8,128)(2,1)} %get-tuple-element.27.f1_hbm, ...), custom_call_target="tpu_custom_call" | custom-call | flops 2684354560 | bytes 16777216 | tf_op jit(solution)/shard_map/cond/branch_0_fun/pallas_call | solution.py:292
  87.3 2.4 %shard_map.69 = (f32[8,256,256]{2,1,0:T(8,128)}, f32[8,256,256]{2,1,0:T(8,128)}) custom-call(bf16[8,256,256]{2,1,0:T(8,128)(2,1)S(1)} %get-tuple-element.44.one, bf16[8,256,256]{2,1,0:T(8,128)(2,1)S(1)} %get-tuple-element.45.two), custom_call_target="tpu_custom_call" | custom-call | tf_op jit(solution)/shard_map/pallas_call | solution.py:332
